TPU v7x, 256 devices: a whole 4x4x8 slice. The times are simulated.
256 devices in a mesh: dp: 8 (over y, core), lang: 32 (over x, z).
Axes of the slice: x: 4, y: 4, z: 8, core: 2. Of those that a mesh axis runs over, the one named last changes fastest.
Arguments:
- inputs: bfloat16 [32768, 2048], P(('dp', 'lang')), may hold values from -6 to 6
- grad_out: bfloat16 [32768, 2048], P(('dp', 'lang')), may hold values from -6 to 6
- lang_ids: int32 [32768], P(('dp', 'lang')), may hold values from 0 to 199, as said below
- lang_block: int32 [200], replicated, may hold values from 0 to 31, as said below
- block_owner: int32 [32], replicated, may hold values from 0 to 31, each once
- w_in: bfloat16 [32, 4096, 2048], P('lang', 'dp'), may hold values from -0.125 to 0.125
- w_out: bfloat16 [32, 4096, 2048], P('lang', 'dp'), may hold values from -0.09375 to 0.09375
Outputs:
- grad_in: bfloat16 [32768, 2048], P(('dp', 'lang'))
- grad_w_in: bfloat16 [32, 4096, 2048], P('lang', 'dp')
- grad_w_out: bfloat16 [32, 4096, 2048], P('lang', 'dp')
Inputs may be any that keep to these rules, and one draw needn't show every extreme that they name: `lang_ids`: through lang_block, the 128 rows of one device name any one block at most 5 times; in every draw one block is named exactly 5 times by the rows of every device. `lang_block`: every block has at least one language. A permutation: block b's weights and gradients sit at index block_owner[b] of the block dimension.
All inputs are finite; a program needn't handle non-finite values.
Results may differ from a plain program's by a relative error of at most 0.019.
Values may be sent and summed in bfloat16 or wider, within the bound.
A program may use at most 128 MiB of HBM per device.

v0:
```python
import math
import jax
import jax.numpy as jnp
from jax import lax
from jax.sharding import PartitionSpec as P

gelu_scale = math.sqrt(2.0 / math.pi)


def gelu_parts(pre_act):
    tanh_arg = gelu_scale * (pre_act + 0.044715 * pre_act * pre_act * pre_act)
    tangent = jnp.tanh(tanh_arg)
    gelu_value = 0.5 * pre_act * (1.0 + tangent)
    gelu_slope = 0.5 * (1.0 + tangent) + 0.5 * pre_act * (1.0 - tangent * tangent) * gelu_scale * (
        1.0 + 3.0 * 0.044715 * pre_act * pre_act
    )
    return (gelu_value, gelu_slope)


def local_grads(gathered, w_first, w_second):
    rows_x = gathered[:, 0]
    rows_g = gathered[:, 1]
    pre_act = jnp.dot(rows_x, w_first.T, preferred_element_type=jnp.float32)
    gelu_value, gelu_slope = gelu_parts(pre_act)
    activated = gelu_value.astype(jnp.bfloat16)
    back_grad = jnp.dot(rows_g, w_second.T, preferred_element_type=jnp.float32)
    pre_grad = (back_grad * gelu_slope).astype(jnp.bfloat16)
    g_out = jnp.dot(activated.T, rows_g, preferred_element_type=jnp.float32).astype(jnp.bfloat16)
    g_in = jnp.dot(pre_grad.T, rows_x, preferred_element_type=jnp.float32).astype(jnp.bfloat16)
    return (pre_grad, g_in, g_out)


def body(inputs, grad_out, lang_ids, lang_block, block_owner, w_in, w_out):
    tok_rows = inputs.shape[0]
    feat_width = inputs.shape[1]
    lang_count = lax.axis_size("lang")
    dp_count = lax.axis_size("dp")
    per_peer = 5 * tok_rows // (4 * lang_count)
    languages = lang_block.shape[0]
    block_count = block_owner.shape[0]
    lang_hits = (lang_ids[:, None] == jnp.arange(languages, dtype=jnp.int32)[None, :]).astype(
        jnp.int32
    )
    row_block = jnp.sum(lang_hits * lang_block[None, :], axis=1)
    block_hits = (row_block[:, None] == jnp.arange(block_count, dtype=jnp.int32)[None, :]).astype(
        jnp.int32
    )
    holder = jnp.sum(block_hits * block_owner[None, :], axis=1)
    holder_hits = (holder[:, None] == jnp.arange(lang_count, dtype=jnp.int32)[None, :]).astype(
        jnp.int32
    )
    earlier = jnp.cumsum(holder_hits, axis=0) - holder_hits
    slot_index = jnp.sum(earlier * holder_hits, axis=1)
    position = holder * per_peer + slot_index
    packed = jnp.stack([inputs, grad_out], axis=1)
    w_first = w_in[0]
    w_second = w_out[0]
    col_rows, col_pos = (
        lax.all_gather(packed[None], "dp", axis=0, tiled=True),
        lax.all_gather(position[None], "dp", axis=0, tiled=True),
    )
    dp_index = jnp.arange(dp_count, dtype=jnp.int32)[:, None]
    target = col_pos // per_peer * (dp_count * per_peer) + dp_index * per_peer + col_pos % per_peer
    outgoing = jnp.zeros((lang_count * dp_count * per_peer, 2, feat_width), jnp.bfloat16)
    outgoing = outgoing.at[target.reshape(-1)].set(col_rows.reshape(-1, 2, feat_width), mode="drop")
    arrived = lax.all_to_all(
        outgoing.reshape(lang_count, dp_count * per_peer, 2, feat_width),
        "lang",
        split_axis=0,
        concat_axis=0,
        tiled=True,
    )
    gathered = arrived.reshape(-1, 2, feat_width)
    pre_grad, g_in, g_out = local_grads(gathered, w_first, w_second)
    partial_dx = jnp.dot(pre_grad, w_first, preferred_element_type=jnp.float32)
    partial_dx = partial_dx.reshape(lang_count, dp_count, per_peer, feat_width)
    summed = (
        lax.psum_scatter(partial_dx.astype(jnp.bfloat16), "dp", scatter_dimension=1, tiled=True)
        .astype(jnp.float32)
        .reshape(lang_count, per_peer, feat_width)
    )
    returned = lax.all_to_all(
        summed.astype(jnp.bfloat16), "lang", split_axis=0, concat_axis=0, tiled=True
    )
    grad_in = returned.reshape(lang_count * per_peer, feat_width)[position]
    return (grad_in, g_in[None], g_out[None])


def solution(mesh):
    in_specs = (
        P(("dp", "lang"), None),
        P(("dp", "lang"), None),
        P(("dp", "lang")),
        P(),
        P(),
        P("lang", "dp", None),
        P("lang", "dp", None),
    )
    out_specs = (P(("dp", "lang"), None), P("lang", "dp", None), P("lang", "dp", None))
    return jax.shard_map(body, mesh=mesh, in_specs=in_specs, out_specs=out_specs, check_vma=False)
```

profile of v0, /device:TPU:25, one launch (start us, length us, event | category | flops | bytes accessed | tf_op | source)
XLA Modules:
  0.0 580.1 jit_solution(14757968906127118816)
XLA Ops:
  7.2 0.0 copy-start
  7.2 0.0 copy-start.2
  7.2 0.0 copy-start.3
  7.2 0.0 copy-start.5
  7.2 0.0 all-gather.5.cloned.1.call-start
  7.3 2.4 pad_maximum_fusion
  9.7 0.0 all-gather.5.cloned.1.call-update
  9.7 0.0 reduce-scatter.2.cloned.1.call-start
  9.7 0.0 copy-done.2
  9.7 0.0 copy-done.3
  9.8 0.1 select_reduce_fusion
  9.9 0.0 copy-done.5
  9.9 0.2 select_reduce_fusion.2
  10.0 0.1 fusion.23
  10.1 0.2 reduce_window_sum.11
  10.3 0.2 select_reduce_fusion.1
  10.5 9.0 %all-gather.2 = s32[8,1,128]{2,1,0:T(1,128)S(1)} all-gather(s32[1,1,128]{2,1,0:T(1,128)S(1)} %fusion.34), channel_id=2, replica_groups=mesh['dp'=8,'lang'=32] {'dp'}, dimensions={0}, use_global_device_ids=true | all-gather | bytes 4608 | tf_op jit(solution)/shard_map/all_gather | solution.py:60
  19.5 0.4 rem.15
  19.8 0.1 fusion.26
  19.9 44.1 %all-gather.5.cloned.1.call-done = bf16[1024,2,2048]{2,0,1:T(8,128)(2,1)} async-done(((bf16[128,2,2048]{2,0,1:T(8,128)(2,1)}), bf16[1024,2,2048]{2,0,1:T(8,128)(2,1)}) %all-gather.5.cloned.1.call-update) | async-done | bytes 8388624 | tf_op jit(solution)/shard_map/all_gather | solution.py:59
  64.0 16.4 %copy.33 = bf16[1024,2,2048]{2,1,0:T(2,128)(2,1)} copy(bf16[1024,2,2048]{2,0,1:T(8,128)(2,1)} %all-gather.5.cloned.1.call-done) | data formatting | bytes 16777216 | tf_op jit(solution)/shard_map/all_gather | solution.py:59
  80.4 6.6 %broadcast_in_dim.8 = bf16[1280,2,2048]{2,1,0:T(2,128)(2,1)} broadcast(bf16[]{:T(256)} %constant.15.clone.1), dimensions={} | broadcast | bytes 10485762 | tf_op jit(solution)/shard_map/broadcast_in_dim | solution.py:64
  87.0 127.9 %scatter_fusion = bf16[1280,2,2048]{2,1,0:T(2,128)(2,1)} fusion(bf16[1280,2,2048]{2,1,0:T(2,128)(2,1)} %broadcast_in_dim.8, s32[1024]{0:T(1024)S(1)} %bitcast.74, bf16[1024,2,2048]{2,1,0:T(2,128)(2,1)} %copy.33), kind=kCustom, calls=%fused_computation.1 | custom fusion | bytes 25169920 | tf_op jit(solution)/shard_map/scatter | solution.py:65
  214.9 237.2 %all_to_all.10 = bf16[32,40,2,2048]{3,2,1,0:T(2,128)(2,1)} all-to-all(bf16[32,40,2,2048]{3,2,1,0:T(2,128)(2,1)} %bitcast.62), channel_id=1, replica_groups=mesh['dp'=8,'lang'=32] {'lang'}, dimensions={0} | all-to-all | bytes 20971520 | tf_op jit(solution)/shard_map/all_to_all | solution.py:66
  452.1 12.9 %copy.34 = bf16[32,40,2,2048]{3,1,0,2:T(8,128)(2,1)} copy(bf16[32,40,2,2048]{3,2,1,0:T(2,128)(2,1)} %all_to_all.10) | data formatting | bytes 20971520 | tf_op jit(solution)/shard_map/all_to_all | solution.py:66
  465.0 0.0 copy-done
  465.0 0.0 copy-start.1
  465.0 0.0 copy-start.4
  465.0 5.2 fusion.3
  470.2 0.0 copy-start.6
  470.3 1.5 copy-done.6
  471.7 0.0 copy-done.1
  471.7 0.0 copy-done.4
  471.7 4.3 fusion.5
  476.0 1.6 dot_general.19
  477.6 4.9 convolution_convert_fusion
  482.5 5.2 copy.36
  487.8 0.0 reduce-scatter.2.cloned.1.call-update
  487.8 42.7 %reduce-scatter.2.cloned.1.call-done = bf16[32,1,5,2048]{3,0,2,1:T(8,128)(2,1)} async-done(((bf16[32,8,5,2048]{3,0,2,1:T(8,128)(2,1)}), bf16[32,1,5,2048]{3,0,2,1:T(8,128)(2,1)}) %reduce-scatter.2.cloned.1.call-update) | async-done | bytes 655376 | tf_op jit(solution)/shard_map/reduce_scatter | solution.py:78
  530.5 2.4 copy.37
  532.9 9.6 %all-to-all-start.1 = ((bf16[32,5,2048]{2,1,0:T(8,128)(2,1)}), bf16[32,5,2048]{2,1,0:T(8,128)(2,1)}, u32[]{:S(2)}, u32[]{:S(2)}) async-start(bf16[32,5,2048]{2,1,0:T(8,128)(2,1)} %copy.37), calls=%async_computation.2 | async-start | bytes 2097152 | tf_op jit(solution)/shard_map/all_to_all | solution.py:82
  542.5 0.0 copy-start.7
  542.6 6.7 %fusion.9 = bf16[1,512,2048]{2,1,0:T(8,128)(2,1)} fusion(bf16[1280,512]{1,0:T(8,128)(2,1)S(1)} %fusion.5, bf16[1280,2,2048]{2,0,1:T(8,128)(2,1)} %bitcast.64), kind=kOutput, calls=%fused_computation.16 | convolution fusion | flops 2685403136 | bytes 8650752 | tf_op jit(solution)/shard_map/dot_general | solution.py:29
  549.3 0.0 copy-done.7
  549.3 6.8 %fusion.8 = bf16[1,512,2048]{2,1,0:T(8,128)(2,1)} fusion(bf16[1280,2,2048]{2,0,1:T(8,128)(2,1)} %bitcast.65, f32[1280,512]{1,0:T(8,128)S(1)} %copy-done.7), kind=kOutput, calls=%fused_computation.15 | convolution fusion | flops 2691301376 | bytes 9961472 | tf_op jit(solution)/shard_map/dot_general | solution.py:28
  556.1 14.0 %all-to-all-done.1 = bf16[32,5,2048]{2,1,0:T(8,128)(2,1)} async-done(((bf16[32,5,2048]{2,1,0:T(8,128)(2,1)}), bf16[32,5,2048]{2,1,0:T(8,128)(2,1)}, u32[]{:S(2)}, u32[]{:S(2)}) %all-to-all-start.1) | async-done | bytes 655392 | tf_op jit(solution)/shard_map/all_to_all | solution.py:82
  570.1 1.5 reshape.110
  571.5 1.7 gather_fusion
  (6 shorter events, 0.0 us)
Async XLA Ops:
  7.2 457.8 %copy-start = (bf16[1,512,2048]{2,1,0:T(8,128)(2,1)S(1)}, bf16[1,512,2048]{2,1,0:T(8,128)(2,1)}, u32[]{:S(2)}) copy-start(bf16[1,512,2048]{2,1,0:T(8,128)(2,1)} %param.12) | copy-start | bytes 6291460
  7.2 2.6 copy-start.2
  7.2 2.6 copy-start.3
  7.2 2.7 copy-start.5
  7.2 56.8 %all-gather.5.cloned.1.call-start = ((), (), s32[]{:S(2)}) async-start(), calls=%async_computation.4 | async-start | bytes 9437184 | tf_op jit(solution)/shard_map/all_gather | solution.py:59
  9.7 520.8 %reduce-scatter.2.cloned.1.call-start = ((), (), s32[]{:S(2)}) async-start(), calls=%async_computation.3 | async-start | bytes 5898240 | tf_op jit(solution)/shard_map/reduce_scatter | solution.py:78
  465.0 6.7 %copy-start.1 = (bf16[32,40,2,2048]{3,1,0,2:T(8,128)(2,1)S(1)}, bf16[32,40,2,2048]{3,1,0,2:T(8,128)(2,1)}, u32[]{:S(2)}) copy-start(bf16[32,40,2,2048]{3,1,0,2:T(8,128)(2,1)} %copy.34) | copy-start | bytes 31457284
  465.0 6.7 %copy-start.4 = (bf16[1,512,2048]{2,1,0:T(8,128)(2,1)S(1)}, bf16[1,512,2048]{2,1,0:T(8,128)(2,1)}, u32[]{:S(2)}) copy-start(bf16[1,512,2048]{2,1,0:T(8,128)(2,1)} %param.13) | copy-start | bytes 6291460
  470.2 1.5 copy-start.6
  532.9 37.2 %all-to-all-start.1 = ((bf16[32,5,2048]{2,1,0:T(8,128)(2,1)}), bf16[32,5,2048]{2,1,0:T(8,128)(2,1)}, u32[]{:S(2)}, u32[]{:S(2)}) async-start(bf16[32,5,2048]{2,1,0:T(8,128)(2,1)} %copy.37), calls=%async_computation.2 | async-start | bytes 2097152 | tf_op jit(solution)/shard_map/all_to_all | solution.py:82
  542.5 6.8 %copy-start.7 = (f32[1280,512]{1,0:T(8,128)S(1)}, f32[1280,512]{1,0:T(8,128)}, u32[]{:S(2)}) copy-start(f32[1280,512]{1,0:T(8,128)} %copy-done.6) | copy-start | bytes 7864324
Sparse Core Ops, SparseCore 0:
  10.5 53.4 all-gather.4
  487.9 42.5 reduce-scatter.1
where the time goes:
time: 582 us; the launch traced here: 580 us
  blocking collectives  246 us (42%)
  local copies, waits for them, and re-layouts  178 us (31%)
  waiting for transfers between devices  101 us (17%)
  matrix products  28 us (5%)
  between operations  14.2 us (2%)
  starting transfers between devices  9.69 us (2%)
    all_to_all x1, blocking collectives, body(): lax.all_to_all(outgoing.reshape(lang_count, dp_count * per_peer, 2, feat_...  237 us
    scatter x1, local copies, waits for them, and re-layouts, body(): outgoing.at[target.reshape(-1)]  128 us
    all_gather x1, waiting for transfers between devices, body(): lax.all_gather(packed[None], 'dp', axis=0, tiled=True)  44.1 us
    reduce_scatter x1, waiting for transfers between devices, body(): lax.psum_scatter(partial_dx.astype(jnp.bfloat16), 'dp', scatter_dimension...  42.7 us
    all_gather x1, local copies, waits for them, and re-layouts, body(): lax.all_gather(packed[None], 'dp', axis=0, tiled=True)  16.4 us
    all_to_all x1, waiting for transfers between devices, body(): lax.all_to_all(summed.astype(jnp.bfloat16), 'lang', split_axis=0, concat_...  14 us
    all_to_all x1, local copies, waits for them, and re-layouts, body(): lax.all_to_all(outgoing.reshape(lang_count, dp_count * per_peer, 2, feat_...  12.9 us
  transfers between devices with their start and end apart: 3, of which 3 were waited for; matrix products, arithmetic and copies ran while one was open for 3% of the time, Pallas kernels for 0%

commit v1 on v0

--- a/solution.py
+++ b/solution.py
@@ -56,7 +56,9 @@
     w_first = w_in[0]
     w_second = w_out[0]
     col_rows, col_pos = (
-        lax.all_gather(packed[None], "dp", axis=0, tiled=True),
+        jnp.concatenate(
+            lax.all_to_all(jnp.stack([packed[None]] * lax.axis_size("dp")), "dp", 0, 0), axis=0
+        ),
         lax.all_gather(position[None], "dp", axis=0, tiled=True),
     )
     dp_index = jnp.arange(dp_count, dtype=jnp.int32)[:, None]

time: 582 us -> 620 us (1.065)
  blocking collectives: 246 us -> 332 us
  waiting for transfers between devices: 101 us -> 55.5 us
  local copies, waits for them, and re-layouts: 178 us -> 169 us
  starting transfers between devices: 9.69 us -> 16.9 us
    all_gather x1, blocking collectives: 8.96 us -> 94.8 us  [body(): lax.all_gather(position[None], 'dp', axis=0, tiled=True)]
    all_gather x1 -> x0, waiting for transfers between devices: 44.1 us -> none  [body(): lax.all_gather(packed[None], 'dp', axis=0, tiled=True)]
    all_gather x1 -> x0, local copies, waits for them, and re-layouts: 16.4 us -> none  [body(): lax.all_gather(packed[None], 'dp', axis=0, tiled=True)]
    another operation x0 -> x2, local copies, waits for them, and re-layouts: none -> 7.62 us  [the longest x1 6.54 us: body(): jnp.stack([packed[None]] * lax.axis_size('dp'))]
    all_to_all x0 -> x1, starting transfers between devices: none -> 7.27 us  [body(): lax.all_to_all(jnp.stack([packed[None]] * lax.axis_size('dp')), 'dp', 0, 0)]
  transfers between devices with their start and end apart: 3 -> 3, of which waited for: 3 -> 2; matrix products, arithmetic and copies ran while one was open for 3% -> 2% of each run, Pallas kernels for 0% -> 0%
where the time goes in v1:
time: 620 us; the launch traced here: 618 us
  blocking collectives  332 us (54%)
  local copies, waits for them, and re-layouts  169 us (27%)
  waiting for transfers between devices  55.5 us (9%)
  matrix products  28 us (5%)
  starting transfers between devices  16.9 us (3%)
  between operations  14.2 us (2%)
    all_to_all x1, blocking collectives, body(): lax.all_to_all(outgoing.reshape(lang_count, dp_count * per_peer, 2, feat_...  237 us
    scatter x1, local copies, waits for them, and re-layouts, body(): outgoing.at[target.reshape(-1)]  128 us
    all_gather x1, blocking collectives, body(): lax.all_gather(position[None], 'dp', axis=0, tiled=True)  94.8 us
    reduce_scatter x1, waiting for transfers between devices, body(): lax.psum_scatter(partial_dx.astype(jnp.bfloat16), 'dp', scatter_dimension...  41.6 us
    all_to_all x1, waiting for transfers between devices, body(): lax.all_to_all(summed.astype(jnp.bfloat16), 'lang', split_axis=0, concat_...  13.9 us
    all_to_all x1, local copies, waits for them, and re-layouts, body(): lax.all_to_all(outgoing.reshape(lang_count, dp_count * per_peer, 2, feat_...  12.9 us
  transfers between devices with their start and end apart: 3, of which 2 were waited for; matrix products, arithmetic and copies ran while one was open for 2% of the time, Pallas kernels for 0%

profile of v1, /device:TPU:25, one launch (start us, length us, event | category | flops | bytes accessed | tf_op | source)
XLA Modules:
  0.0 617.9 jit_solution(6312208255353102019)
XLA Ops:
  7.2 0.0 copy-start
  7.2 1.4 pad_maximum_fusion
  8.6 1.1 copy.40
  9.7 6.5 %stack.15 = bf16[8,1,128,2,2048]{4,3,2,1,0:T(2,128)(2,1)} broadcast(bf16[128,2,2048]{2,1,0:T(2,128)(2,1)S(1)} %copy.40), dimensions={2,3,4} | broadcast | bytes 9437184 | tf_op jit(solution)/shard_map/stack | solution.py:60
  16.3 0.0 copy-start.2
  16.3 0.0 copy-start.3
  16.3 0.0 copy-start.5
  16.3 7.3 %all-to-all-start = ((bf16[8,1,128,2,2048]{4,3,2,1,0:T(2,128)(2,1)}), bf16[8,1,128,2,2048]{4,3,2,1,0:T(2,128)(2,1)}, u32[]{:S(2)}, u32[]{:S(2)}) async-start(bf16[8,1,128,2,2048]{4,3,2,1,0:T(2,128)(2,1)} %stack.15), calls=%async_computation | async-start | bytes 16777216 | tf_op jit(solution)/shard_map/all_to_all | solution.py:60
  23.5 0.0 reduce-scatter.2.cloned.1.call-start
  23.5 0.0 copy-done.2
  23.5 0.0 copy-done.3
  23.6 0.1 select_reduce_fusion
  23.7 0.0 copy-done.5
  23.7 0.2 select_reduce_fusion.2
  23.8 0.1 fusion.23
  23.9 0.2 reduce_window_sum.11
  24.1 0.2 select_reduce_fusion.1
  24.3 94.8 %all-gather.1 = s32[8,1,128]{2,1,0:T(1,128)S(1)} all-gather(s32[1,1,128]{2,1,0:T(1,128)S(1)} %fusion.34), channel_id=2, replica_groups=mesh['dp'=8,'lang'=32] {'dp'}, dimensions={0}, use_global_device_ids=true | all-gather | bytes 4608 | tf_op jit(solution)/shard_map/all_gather | solution.py:62
  119.1 0.4 rem.15
  119.5 0.1 fusion.26
  119.6 0.0 all-to-all-done
  119.6 6.6 %broadcast_in_dim.6 = bf16[1280,2,2048]{2,1,0:T(2,128)(2,1)} broadcast(bf16[]{:T(256)} %constant.15.clone.1), dimensions={} | broadcast | bytes 10485762 | tf_op jit(solution)/shard_map/broadcast_in_dim | solution.py:66
  126.2 127.9 %scatter_fusion = bf16[1280,2,2048]{2,1,0:T(2,128)(2,1)} fusion(bf16[1280,2,2048]{2,1,0:T(2,128)(2,1)} %broadcast_in_dim.6, s32[1024]{0:T(1024)S(1)} %bitcast.75, bf16[1024,2,2048]{2,1,0:T(2,128)(2,1)} %bitcast.11), kind=kCustom, calls=%fused_computation.1 | custom fusion | bytes 25169920 | tf_op jit(solution)/shard_map/scatter | solution.py:67
  254.1 236.9 %all_to_all.15 = bf16[32,40,2,2048]{3,2,1,0:T(2,128)(2,1)} all-to-all(bf16[32,40,2,2048]{3,2,1,0:T(2,128)(2,1)} %bitcast.63), channel_id=1, replica_groups=mesh['dp'=8,'lang'=32] {'lang'}, dimensions={0} | all-to-all | bytes 20971520 | tf_op jit(solution)/shard_map/all_to_all | solution.py:68
  491.0 12.9 %copy.41 = bf16[32,40,2,2048]{3,1,0,2:T(8,128)(2,1)} copy(bf16[32,40,2,2048]{3,2,1,0:T(2,128)(2,1)} %all_to_all.15) | data formatting | bytes 20971520 | tf_op jit(solution)/shard_map/all_to_all | solution.py:68
  503.9 0.0 copy-done
  503.9 0.0 copy-start.1
  503.9 0.0 copy-start.4
  503.9 5.2 fusion.3
  509.1 0.0 copy-start.6
  509.2 1.5 copy-done.6
  510.6 0.0 copy-done.1
  510.6 0.0 copy-done.4
  510.6 4.3 fusion.5
  514.9 1.6 dot_general.19
  516.5 4.9 convolution_convert_fusion
  521.4 5.2 copy.43
  526.7 0.0 reduce-scatter.2.cloned.1.call-update
  526.7 41.6 %reduce-scatter.2.cloned.1.call-done = bf16[32,1,5,2048]{3,0,2,1:T(8,128)(2,1)} async-done(((bf16[32,8,5,2048]{3,0,2,1:T(8,128)(2,1)}), bf16[32,1,5,2048]{3,0,2,1:T(8,128)(2,1)}) %reduce-scatter.2.cloned.1.call-update) | async-done | bytes 655376 | tf_op jit(solution)/shard_map/reduce_scatter | solution.py:80
  568.3 2.4 copy.44
  570.8 9.6 %all-to-all-start.2 = ((bf16[32,5,2048]{2,1,0:T(8,128)(2,1)}), bf16[32,5,2048]{2,1,0:T(8,128)(2,1)}, u32[]{:S(2)}, u32[]{:S(2)}) async-start(bf16[32,5,2048]{2,1,0:T(8,128)(2,1)} %copy.44), calls=%async_computation.3 | async-start | bytes 2097152 | tf_op jit(solution)/shard_map/all_to_all | solution.py:84
  580.4 0.0 copy-start.7
  580.4 6.7 %fusion.9 = bf16[1,512,2048]{2,1,0:T(8,128)(2,1)} fusion(bf16[1280,512]{1,0:T(8,128)(2,1)S(1)} %fusion.5, bf16[1280,2,2048]{2,0,1:T(8,128)(2,1)} %bitcast.65), kind=kOutput, calls=%fused_computation.16 | convolution fusion | flops 2685403136 | bytes 8650752 | tf_op jit(solution)/shard_map/dot_general | solution.py:29
  587.2 0.0 copy-done.7
  587.2 6.8 %fusion.8 = bf16[1,512,2048]{2,1,0:T(8,128)(2,1)} fusion(bf16[1280,2,2048]{2,0,1:T(8,128)(2,1)} %bitcast.66, f32[1280,512]{1,0:T(8,128)S(1)} %copy-done.7), kind=kOutput, calls=%fused_computation.15 | convolution fusion | flops 2691301376 | bytes 9961472 | tf_op jit(solution)/shard_map/dot_general | solution.py:28
  594.0 13.9 %all-to-all-done.2 = bf16[32,5,2048]{2,1,0:T(8,128)(2,1)} async-done(((bf16[32,5,2048]{2,1,0:T(8,128)(2,1)}), bf16[32,5,2048]{2,1,0:T(8,128)(2,1)}, u32[]{:S(2)}, u32[]{:S(2)}) %all-to-all-start.2) | async-done | bytes 655392 | tf_op jit(solution)/shard_map/all_to_all | solution.py:84
  607.9 1.5 reshape.108
  609.4 1.7 gather_fusion
  (6 shorter events, 0.0 us)
Async XLA Ops:
  7.2 496.7 %copy-start = (bf16[1,512,2048]{2,1,0:T(8,128)(2,1)S(1)}, bf16[1,512,2048]{2,1,0:T(8,128)(2,1)}, u32[]{:S(2)}) copy-start(bf16[1,512,2048]{2,1,0:T(8,128)(2,1)} %param.12) | copy-start | bytes 6291460
  16.3 7.3 %copy-start.2 = (s32[200]{0:T(256)S(1)}, s32[200]{0:T(256)}, u32[]{:S(2)}) copy-start(s32[200]{0:T(256)} %param.10) | copy-start | bytes 2404
  16.3 7.3 %copy-start.3 = (s32[128]{0:T(128)S(1)}, s32[128]{0:T(128)}, u32[]{:S(2)}) copy-start(s32[128]{0:T(128)} %param.9) | copy-start | bytes 1540
  16.3 7.4 %copy-start.5 = (s32[32]{0:T(128)S(1)}, s32[32]{0:T(128)}, u32[]{:S(2)}) copy-start(s32[32]{0:T(128)} %param.11) | copy-start | bytes 388
  16.3 103.3 %all-to-all-start = ((bf16[8,1,128,2,2048]{4,3,2,1,0:T(2,128)(2,1)}), bf16[8,1,128,2,2048]{4,3,2,1,0:T(2,128)(2,1)}, u32[]{:S(2)}, u32[]{:S(2)}) async-start(bf16[8,1,128,2,2048]{4,3,2,1,0:T(2,128)(2,1)} %stack.15), calls=%async_computation | async-start | bytes 16777216 | tf_op jit(solution)/shard_map/all_to_all | solution.py:60
  23.5 544.8 %reduce-scatter.2.cloned.1.call-start = ((), (), s32[]{:S(2)}) async-start(), calls=%async_computation.4 | async-start | bytes 5898240 | tf_op jit(solution)/shard_map/reduce_scatter | solution.py:80
  503.9 6.7 %copy-start.1 = (bf16[32,40,2,2048]{3,1,0,2:T(8,128)(2,1)S(1)}, bf16[32,40,2,2048]{3,1,0,2:T(8,128)(2,1)}, u32[]{:S(2)}) copy-start(bf16[32,40,2,2048]{3,1,0,2:T(8,128)(2,1)} %copy.41) | copy-start | bytes 31457284
  503.9 6.7 %copy-start.4 = (bf16[1,512,2048]{2,1,0:T(8,128)(2,1)S(1)}, bf16[1,512,2048]{2,1,0:T(8,128)(2,1)}, u32[]{:S(2)}) copy-start(bf16[1,512,2048]{2,1,0:T(8,128)(2,1)} %param.13) | copy-start | bytes 6291460
  509.1 1.5 copy-start.6
  570.8 37.1 %all-to-all-start.2 = ((bf16[32,5,2048]{2,1,0:T(8,128)(2,1)}), bf16[32,5,2048]{2,1,0:T(8,128)(2,1)}, u32[]{:S(2)}, u32[]{:S(2)}) async-start(bf16[32,5,2048]{2,1,0:T(8,128)(2,1)} %copy.44), calls=%async_computation.3 | async-start | bytes 2097152 | tf_op jit(solution)/shard_map/all_to_all | solution.py:84
  580.4 6.8 %copy-start.7 = (f32[1280,512]{1,0:T(8,128)S(1)}, f32[1280,512]{1,0:T(8,128)}, u32[]{:S(2)}) copy-start(f32[1280,512]{1,0:T(8,128)} %copy-done.6) | copy-start | bytes 7864324
Sparse Core Ops, SparseCore 0:
  526.8 41.4 reduce-scatter.1
